TPU v7x, 32 devices: a whole 2x2x4 slice. The times are simulated.
32 devices in a mesh: row: 8 (over y, x, core), col: 4 (over z).
Axes of the slice: x: 2, y: 2, z: 4, core: 2. Of those that a mesh axis runs over, the one named last changes fastest.
Arguments:
- slab_u: bfloat16 [16, 4, 1408, 256], P('row', 'col'), may hold values from -6 to 6
- slab_v: bfloat16 [16, 4, 1408, 256], P('row', 'col'), may hold values from -0.15625 to 0.15625
- slab_rank: int32 [16, 4], P('row', 'col'), may hold values from 42 to 256, as said below
- panel_u: bfloat16 [2, 16, 1408, 256], P(None, 'row', 'col'), may hold values from -6 to 6
- panel_v: bfloat16 [2, 16, 1408, 256], P(None, 'row', 'col'), may hold values from -0.15625 to 0.15625
- panel_rank: int32 [2, 16], P(None, 'row'), may hold values from 42 to 256, as said below
- inverse_block: bfloat16 [2, 1408, 1408], P(None, 'col'), as said below
- column_tiles: int32 [4], P('col'), may hold values from 0 to 15, as said below
- sketch: bfloat16 [1408, 256], replicated, may hold values from -0.15625 to 0.15625
Outputs:
- basis_out: bfloat16 [16, 4, 1408, 256], P('row', 'col')
- coeff_out: bfloat16 [16, 4, 1408, 256], P('row', 'col')
Inputs may be any that keep to these rules, and one draw needn't show every extreme that they name: `slab_rank`: columns of a slab tile's left factor at or past its rank are ignored. `panel_rank`: columns of a panel tile's left factor at or past its rank are ignored. `column_tiles`: entries are distinct tile rows of the slab. `inverse_block`: each block is lower triangular with a positive diagonal.
All inputs are finite; a program needn't handle non-finite values.
Results may differ from a plain program's by a relative error of at most 0.015.
Values may be sent and summed in bfloat16 or wider, within the bound.
A program may use at most 128 MiB of HBM per device.

v0:
```python
import jax
import jax.numpy as jnp
from jax import lax
from jax.sharding import PartitionSpec as P


def spread(array, axis, root):
    mine = lax.axis_index(axis) == root
    return lax.psum(jnp.where(mine, array, jnp.zeros_like(array)), axis)


def mask_columns(factor, rank):
    columns = jnp.arange(factor.shape[-1], dtype=jnp.int32)
    keep = (columns < rank).astype(factor.dtype)
    return factor * keep


def update_tile(tile_u, tile_v, tile_rank, row_u, row_v, side_u, side_v, sketch):
    masked_slab = mask_columns(tile_u, tile_rank)
    lefts = [masked_slab]
    rights = [tile_v]
    for panel in range(row_u.shape[0]):
        cross = jnp.dot(row_v[panel].T, side_v[panel], preferred_element_type=jnp.float32).astype(
            jnp.bfloat16
        )
        update = jnp.dot(side_u[panel], cross.T, preferred_element_type=jnp.float32).astype(
            jnp.bfloat16
        )
        lefts.append(row_u[panel])
        rights.append(-update)
    left_cat = jnp.concatenate(lefts, axis=1)
    right_cat = jnp.concatenate(rights, axis=1)
    small = jnp.dot(right_cat.T, sketch, preferred_element_type=jnp.float32).astype(jnp.bfloat16)
    image = jnp.dot(left_cat, small, preferred_element_type=jnp.float32)
    gram = jnp.dot(
        image.T, image, precision=lax.Precision.HIGHEST, preferred_element_type=jnp.float32
    )
    gram = gram + jnp.eye(gram.shape[0], dtype=jnp.float32)
    factor = jnp.linalg.cholesky(gram)
    basis = lax.linalg.triangular_solve(
        factor, image, left_side=False, lower=True, transpose_a=True
    )
    scale_basis = jnp.sqrt(jnp.float32(tile_u.shape[0]))
    basis_out = (basis * scale_basis).astype(jnp.bfloat16)
    basis_low = basis.astype(jnp.bfloat16)
    project = jnp.dot(left_cat.T, basis_low, preferred_element_type=jnp.float32).astype(
        jnp.bfloat16
    )
    coeff_out = jnp.dot(right_cat, project, preferred_element_type=jnp.float32).astype(jnp.bfloat16)
    return (basis_out, coeff_out)


def shards(
    slab_u, slab_v, slab_rank, panel_u, panel_v, panel_rank, inverse_block, column_tiles, sketch
):
    rows_here = panel_u.shape[1]
    masked_panel = mask_columns(panel_u, panel_rank[:, :, None, None])
    whole_inverse = lax.all_gather(inverse_block, "col", axis=1, tiled=True)
    whole_u, raw_v = (
        lax.all_gather(masked_panel, "col", axis=2, tiled=True),
        lax.all_gather(panel_v, "col", axis=2, tiled=True),
    )
    whole_v = jnp.einsum(
        "pab,ptbr->ptar", whole_inverse, raw_v, preferred_element_type=jnp.float32
    ).astype(jnp.bfloat16)
    col_local = 0
    target = column_tiles[col_local]
    owner = target // rows_here
    local_index = target - owner * rows_here
    pick_u = lax.dynamic_index_in_dim(whole_u, local_index, 1, keepdims=False)
    pick_v = lax.dynamic_index_in_dim(whole_v, local_index, 1, keepdims=False)
    stacked = jnp.stack([pick_u, pick_v])
    side_list = [spread(stacked, "row", owner)]
    basis_rows = []
    coeff_rows = []
    for row_local in range(rows_here):
        col_local = 0
        side = side_list[col_local]
        basis_tile, coeff_tile = update_tile(
            slab_u[row_local, col_local],
            slab_v[row_local, col_local],
            slab_rank[row_local, col_local],
            whole_u[:, row_local],
            whole_v[:, row_local],
            side[0],
            side[1],
            sketch,
        )
        basis_cols = [basis_tile]
        coeff_cols = [coeff_tile]
        basis_rows.append(jnp.stack(basis_cols))
        coeff_rows.append(jnp.stack(coeff_cols))
    return (jnp.stack(basis_rows), jnp.stack(coeff_rows))


def solution(mesh):
    in_specs = (
        P("row", "col", None, None),
        P("row", "col", None, None),
        P("row", "col"),
        P(None, "row", "col", None),
        P(None, "row", "col", None),
        P(None, "row"),
        P(None, "col", None),
        P("col"),
        P(),
    )
    out_specs = (P("row", "col", None, None), P("row", "col", None, None))
    return jax.shard_map(shards, mesh=mesh, in_specs=in_specs, out_specs=out_specs, check_vma=False)
```

profile of v0, /device:TPU:0, one launch (start us, length us, event | category | flops | bytes accessed | tf_op | source)
XLA Modules:
  0.0 532.9 jit_solution(14474701992062829285)
XLA Ops:
  8.0 2.0 broadcast_multiply_fusion
  12.3 1.4 fusion.51
  13.7 1.1 copy.22
  15.2 56.9 %all-gather.4.cloned.1.call-done = bf16[2,2,1408,256]{3,2,1,0:T(8,128)(2,1)} async-done(((bf16[2,2,352,256]{3,2,1,0:T(8,128)(2,1)}), bf16[2,2,1408,256]{3,2,1,0:T(8,128)(2,1)}) %all-gather.4.cloned.1.call-update) | async-done | bytes 2883600 | tf_op jit(solution)/shard_map/all_gather | solution.py:60
  72.1 1.5 constant_dynamic-slice_fusion.2
  73.5 1.5 copy.12
  75.1 56.5 %all-gather.6.cloned.1.call-done = bf16[2,2,1408,256]{3,2,1,0:T(8,128)(2,1)} async-done(((bf16[2,2,352,256]{3,2,1,0:T(8,128)(2,1)}), bf16[2,2,1408,256]{3,2,1,0:T(8,128)(2,1)}) %all-gather.6.cloned.1.call-update) | async-done | bytes 2883600 | tf_op jit(solution)/shard_map/all_gather | solution.py:61
  131.5 142.5 %all-gather.8.cloned.1.call-done = bf16[2,1408,1408]{2,1,0:T(8,128)(2,1)} async-done(((bf16[2,352,1408]{2,1,0:T(8,128)(2,1)}), bf16[2,1408,1408]{2,1,0:T(8,128)(2,1)}) %all-gather.8.cloned.1.call-update) | async-done | bytes 7929872 | tf_op jit(solution)/shard_map/all_gather | solution.py:58
  274.0 9.5 %fusion.2 = bf16[2,2,256,1408]{3,2,1,0:T(8,128)(2,1)S(1)} fusion(bf16[2,2,1408,256]{3,2,1,0:T(8,128)(2,1)} %all-gather.6.cloned.1.call-done, bf16[2,1408,1408]{2,1,0:T(8,128)(2,1)} %all-gather.8.cloned.1.call-done), kind=kOutput, calls=%fused_computation.6 | convolution fusion | flops 4061528064 | bytes 13697024 | tf_op jit(solution)/shard_map/pab,ptbr->ptar/dot_general | solution.py:63
  283.7 1.4 copy-done.5
  285.1 0.8 copy-done.2
  286.0 2.1 maximum_select_fusion
  289.3 1.4 compare_convert_fusion.1
  290.7 1.2 bitcast_multiply_fusion.1
  291.9 1.6 slice_bitcast_fusion.19
  293.6 59.9 %all-reduce.3.cloned.1.call-done = bf16[2,2,1408,256]{2,3,1,0:T(8,128)(2,1)} async-done(((bf16[2,2,1408,256]{2,3,1,0:T(8,128)(2,1)}), bf16[2,2,1408,256]{2,3,1,0:T(8,128)(2,1)}) %all-reduce.3.cloned.1.call-update) | async-done | bytes 2883600 | tf_op jit(solution)/shard_map/psum | solution.py:9
  353.4 3.5 fusion.8
  356.9 3.5 fusion.7
  360.3 4.4 fusion.14
  364.8 2.4 convolution_add_fusion
  367.4 11.7 %cholesky.164 = f32[128,128]{1,0:T(8,128)S(1)} custom-call(f32[128,128]{1,0:T(8,128)S(1)} %cholesky.197), custom_call_target="Cholesky" | custom-call | tf_op jit(solution)/shard_map/jit(cholesky)/cholesky | solution.py:39
  379.8 10.2 %custom-call.15 = f32[1,128,128]{1,2,0:T(8,128)S(1)} custom-call(f32[1,128,128]{2,1,0:T(8,128)S(1)} %get-tuple-element.57), custom_call_target="InvertDiagBlocksLowerTriangular" | custom-call | tf_op jit(solution)/shard_map/jit(cholesky)/cholesky | solution.py:39
  390.6 11.7 %cholesky.181 = f32[128,128]{1,0:T(8,128)S(1)} custom-call(f32[128,128]{1,0:T(8,128)S(1)} %convolution_subtract_fusion.2), custom_call_target="Cholesky" | custom-call | tf_op jit(solution)/shard_map/jit(cholesky)/cholesky | solution.py:39
  404.5 4.1 while.5
  405.1 1.4 bitcast_dynamic-update-slice_fusion.5
  407.1 1.4 bitcast_dynamic-update-slice_fusion.5
  408.6 19.7 %custom-call.16 = f32[2,128,128]{1,2,0:T(8,128)S(1)} custom-call(f32[2,128,128]{2,1,0:T(8,128)S(1)} %get-tuple-element.19), custom_call_target="InvertDiagBlocksLowerTriangular" | custom-call | tf_op jit(solution)/shard_map/triangular_solve/custom-call.0 | solution.py:40
  428.2 0.8 fusion.21
  429.1 1.3 convolution_subtract_fusion
  431.2 5.7 %fusion.10 = bf16[1,1,1408,256]{3,2,1,0:T(8,128)(2,1)} fusion(bf16[1408,256]{0,1:T(8,128)(2,1)} %fusion.8, bf16[1408,256]{0,1:T(8,128)(2,1)} %fusion.7, bf16[1408,256]{0,1:T(8,128)(2,1)} %bitcast.162, bf16[1408,256]{1,0:T(8,128)(2,1)} %get-tuple-element.43, bf16[1408,256]{1,0:T(8,128)(2,1)} %get-tuple-element.44, bf16[1408,256]{1,0:T(8,128)(2,1)} %get-tuple-element.47, ...), kind=kOutput, calls=%fused_computation.21 | convolution fusion | flops 1122271232 | bytes 6488064 | tf_op jit(solution)/shard_map/dot_general | solution.py:49
  436.9 1.0 fusion.20
  437.9 3.5 fusion.6
  441.3 3.6 fusion.5
  444.9 4.4 fusion.13
  449.4 2.4 convolution_add_fusion.1
  452.0 11.9 %cholesky.130 = f32[128,128]{1,0:T(8,128)S(1)} custom-call(f32[128,128]{1,0:T(8,128)S(1)} %cholesky.194), custom_call_target="Cholesky" | custom-call | tf_op jit(solution)/shard_map/jit(cholesky)/cholesky | solution.py:39
  464.6 9.8 %custom-call.13 = f32[1,128,128]{1,2,0:T(8,128)S(1)} custom-call(f32[1,128,128]{2,1,0:T(8,128)S(1)} %get-tuple-element.53), custom_call_target="InvertDiagBlocksLowerTriangular" | custom-call | tf_op jit(solution)/shard_map/jit(cholesky)/cholesky | solution.py:39
  474.9 11.7 %cholesky.147 = f32[128,128]{1,0:T(8,128)S(1)} custom-call(f32[128,128]{1,0:T(8,128)S(1)} %convolution_subtract_fusion.3), custom_call_target="Cholesky" | custom-call | tf_op jit(solution)/shard_map/jit(cholesky)/cholesky | solution.py:39
  488.6 3.9 while.4
  489.2 1.3 bitcast_dynamic-update-slice_fusion.4
  491.2 1.3 bitcast_dynamic-update-slice_fusion.4
  492.5 19.9 %custom-call.14 = f32[2,128,128]{1,2,0:T(8,128)S(1)} custom-call(f32[2,128,128]{2,1,0:T(8,128)S(1)} %get-tuple-element.18), custom_call_target="InvertDiagBlocksLowerTriangular" | custom-call | tf_op jit(solution)/shard_map/triangular_solve/custom-call.0 | solution.py:40
  512.4 0.8 fusion.23
  513.3 1.3 convolution_subtract_fusion.1
  515.4 5.6 %fusion.9 = bf16[1,1,1408,256]{3,2,1,0:T(8,128)(2,1)} fusion(bf16[1408,256]{0,1:T(8,128)(2,1)} %fusion.6, bf16[1408,256]{0,1:T(8,128)(2,1)} %fusion.5, bf16[1408,256]{0,1:T(8,128)(2,1)} %bitcast.159, bf16[1408,256]{1,0:T(8,128)(2,1)} %get-tuple-element.45, bf16[1408,256]{1,0:T(8,128)(2,1)} %get-tuple-element.42, bf16[1408,256]{1,0:T(8,128)(2,1)} %get-tuple-element.46, ...), kind=kOutput, calls=%fused_computation.20 | convolution fusion | flops 1122271232 | bytes 6488064 | tf_op jit(solution)/shard_map/dot_general | solution.py:49
  521.1 1.0 copy-done.3
  522.3 1.6 copy.18
  523.8 2.3 pad_maximum_fusion.7
  (67 shorter events, 12.7 us)
Async XLA Ops:
  7.2 353.2 %copy-start = (bf16[1408,256]{1,0:T(8,128)(2,1)S(1)}, bf16[1408,256]{1,0:T(8,128)(2,1)}, u32[]{:S(2)}) copy-start(bf16[1408,256]{1,0:T(8,128)(2,1)} %param.20) | copy-start | bytes 2162692
  7.2 64.9 %all-gather.4.cloned.1.call-start = ((), (), s32[]{:S(2)}) async-start(), calls=%async_computation | async-start | bytes 3604480 | tf_op jit(solution)/shard_map/all_gather | solution.py:60
  10.1 121.5 %all-gather.6.cloned.1.call-start = ((), (), s32[]{:S(2)}) async-start(), calls=%async_computation.1 | async-start | bytes 3604480 | tf_op jit(solution)/shard_map/all_gather | solution.py:61
  10.8 263.2 %all-gather.8.cloned.1.call-start = ((), (), s32[]{:S(2)}) async-start(), calls=%async_computation.2 | async-start | bytes 9912320 | tf_op jit(solution)/shard_map/all_gather | solution.py:58
  11.6 341.9 %all-reduce.3.cloned.1.call-start = ((), (), s32[]{:S(2)}) async-start(), calls=%async_computation.3 | async-start | bytes 5767168 | tf_op jit(solution)/shard_map/psum | solution.py:9
  15.2 345.1 %copy-start.7 = (bf16[1,1,1408,256]{2,3,1,0:T(8,128)(2,1)}, bf16[1,1,1408,256]{2,3,1,0:T(8,128)(2,1)S(1)}, u32[]{:S(2)}) copy-start(bf16[1,1,1408,256]{2,3,1,0:T(8,128)(2,1)S(1)} %copy.23) | copy-start | bytes 2162692
  283.6 1.6 copy-start.5
  283.6 2.4 copy-start.2
  288.1 0.7 copy-start.9
  288.1 2.6 copy-start.4
  288.1 3.8 copy-start.1
  441.3 3.6 copy-start.6
  521.0 1.1 copy-start.3
  522.2 1.6 copy-start.8
Sparse Core Ops, SparseCore 0:
  10.2 61.8 all-gather.3
  73.6 57.8 all-gather.5
  133.1 140.8 all-gather.7
  288.2 65.1 all-reduce.2
where the time goes:
time: 537 us; the launch traced here: 533 us
  waiting for transfers between devices  317 us (59%)
  other arithmetic  121 us (23%)
  matrix products  55.4 us (10%)
  local copies, waits for them, and re-layouts  21.9 us (4%)
  between operations  17.6 us (3%)
    all_gather x1, waiting for transfers between devices, shards(): whole_inverse = lax.all_gather(inverse_block, 'col', axis=1, tiled=True)  142 us
    another operation x14, other arithmetic, update_tile(): factor = jnp.linalg.cholesky(gram)  69.9 us
    psum x1, waiting for transfers between devices, spread(): return lax.psum(jnp.where(mine, array, jnp.zeros_like(array)), axis)  59.9 us
    all_gather x1, waiting for transfers between devices, shards(): lax.all_gather(masked_panel, 'col', axis=2, tiled=True)  56.9 us
    all_gather x1, waiting for transfers between devices, shards(): lax.all_gather(panel_v, 'col', axis=2, tiled=True)  56.5 us
    another operation x5, other arithmetic, update_tile(): lax.linalg.triangular_solve(factor, image, left_side=False, lower=True, t...  39.6 us
    dot_general x4, matrix products, update_tile(): jnp.dot(side_u[panel], cross.T, preferred_element_type=jnp.float32)  14 us
    dot_general x2, matrix products, update_tile(): jnp.dot(right_cat, project, preferred_element_type=jnp.float32)  11.2 us
  transfers between devices with their start and end apart: 4, of which 4 were waited for; matrix products, arithmetic and copies ran while one was open for 2% of the time, Pallas kernels for 0%

commit v1 on v0

v1 whole, which is shorter than its diff:
```python
import jax
import jax.numpy as jnp
from jax import lax
from jax.experimental import pallas as pl
from jax.experimental.pallas import tpu as pltpu
from jax.sharding import PartitionSpec as P

F32 = jnp.float32
BF16 = jnp.bfloat16
GROUP = 4
BLOCK = 128


def mask_columns(factor, rank):
    columns = jnp.arange(factor.shape[-1], dtype=jnp.int32)
    keep = (columns < rank).astype(factor.dtype)
    return factor * keep


def invert_blocks(blocks):
    n = blocks[0].shape[0]
    lane_row = lax.broadcasted_iota(jnp.int32, (1, n), 1)
    many = range(len(blocks))
    left = list(blocks)
    done = [[] for _ in many]
    top = 0
    for j in range(0, n, GROUP):
        start = (j // 8) * 8
        if start > top:
            left = [t[start - top :] for t in left]
            top = start
        rows = n - top
        at = j - top
        row_index = lax.broadcasted_iota(jnp.int32, (rows, n), 0) + top
        lane = lax.broadcasted_iota(jnp.int32, (rows, n), 1)
        inside = (lane >= j) & (lane < j + GROUP)
        for b in many:
            t = left[b]
            col = [
                jnp.broadcast_to(t[:, j + s : j + s + 1], (rows, n)) for s in range(GROUP)
            ]
            row = [t[at + s : at + s + 1, :] for s in range(GROUP)]
            new = jnp.where(inside, 0.0, t)
            for s in range(GROUP):
                pivot = col[s][at + s : at + s + 1, :]
                comb = jnp.where(lane_row == j + s, 1.0, row[s])
                times = jnp.where(row_index > j + s, col[s] / pivot, 0.0)
                for u in range(s + 1, GROUP):
                    col[u] = col[u] - times * col[u][at + s : at + s + 1, :]
                    here = jnp.where(lane_row == j + s, 0.0, row[u])
                    row[u] = here - times[at + u : at + u + 1, :] * comb
                later = (lane_row > j + s) & (lane_row < j + GROUP)
                new = new - times * jnp.where(later, 0.0, comb)
                done[b].append(
                    jnp.where(lane_row <= j + s, comb, 0.0) * lax.rsqrt(pivot)
                )
            left[b] = new
    return [jnp.concatenate(rows_of, axis=0) for rows_of in done]


def full_dot(a, b, dims):
    return lax.dot_general(
        a, b, (dims, ((), ())), precision=lax.Precision.HIGHEST, preferred_element_type=F32
    )


def factor_kernel(gram_ref, out_ref):
    tiles = gram_ref.shape[0]
    n = gram_ref.shape[1]
    half = n // 2
    many = range(tiles)
    first = invert_blocks([gram_ref[b, :half, :half] for b in many])
    lower = [full_dot(gram_ref[b, half:, :half], first[b], ((1,), (1,))) for b in many]
    rest = [
        gram_ref[b, half:, half:] - full_dot(lower[b], lower[b], ((1,), (1,))) for b in many
    ]
    second = invert_blocks(rest)
    for b in many:
        corner = full_dot(lower[b], first[b], ((1,), (0,)))
        out_ref[b, :half, :half] = first[b]
        out_ref[b, :half, half:] = jnp.zeros((half, half), F32)
        out_ref[b, half:, :half] = -full_dot(second[b], corner, ((1,), (0,)))
        out_ref[b, half:, half:] = second[b]


def invert_factor(gram):
    tiles, n, _ = gram.shape
    step = 2 if tiles % 2 == 0 else 1
    return pl.pallas_call(
        factor_kernel,
        grid=(tiles // step,),
        out_shape=jax.ShapeDtypeStruct(gram.shape, F32),
        in_specs=[pl.BlockSpec((step, n, n), lambda i: (i, 0, 0))],
        out_specs=pl.BlockSpec((step, n, n), lambda i: (i, 0, 0)),
        compiler_params=pltpu.CompilerParams(vmem_limit_bytes=32 * 1024 * 1024),
        cost_estimate=pl.CostEstimate(
            flops=tiles * n * n * n, bytes_accessed=2 * gram.size * 4, transcendentals=0
        ),
    )(gram)


def dot(spec, a, b):
    return jnp.einsum(spec, a, b, preferred_element_type=F32)


def shards(
    slab_u, slab_v, slab_rank, panel_u, panel_v, panel_rank, inverse_block, column_tiles, sketch
):
    rows_here = panel_u.shape[1]
    panels = panel_u.shape[0]
    width = sketch.shape[0]
    me = lax.axis_index("row")
    targets = lax.all_gather(column_tiles, "col", axis=0, tiled=True)
    raw_v = lax.all_gather(panel_v, "col", axis=2, tiled=True)
    masked_panel = mask_columns(panel_u, panel_rank[:, :, None, None])
    solved = dot("pab,ptbr->tpar", inverse_block, raw_v).astype(BF16)
    owner = targets // rows_here
    local = targets - owner * rows_here
    sides = jnp.where(
        (owner == me)[:, None, None, None], jnp.take(solved, local, axis=0), jnp.zeros((), BF16)
    )
    side_v = lax.psum(sides, "row")
    part = dot("tpar,cpas->ctprs", solved, side_v).astype(BF16)
    cross = lax.psum_scatter(part, "col", scatter_dimension=0, tiled=True)[0]
    whole_u = lax.all_gather(masked_panel, "col", axis=2, tiled=True)
    target = column_tiles[0]
    mine = target // rows_here
    pick_u = lax.dynamic_index_in_dim(
        whole_u, target - mine * rows_here, 1, keepdims=False
    )
    side_u = lax.psum(jnp.where(mine == me, pick_u, jnp.zeros_like(pick_u)), "row")

    side_small = dot("pas,ak->psk", side_u, sketch).astype(BF16)
    tile_u = slab_u[:, 0]
    tile_v = slab_v[:, 0]
    tile_u = mask_columns(tile_u, slab_rank[:, 0][:, None, None])
    small_v = dot("tar,ak->trk", tile_v, sketch).astype(BF16)
    small_u = (-dot("tprs,psk->tprk", cross, side_small)).astype(BF16)
    image = dot("tar,trk->tak", tile_u, small_v)
    for p in range(panels):
        image = image + dot("tar,trk->tak", whole_u[p], small_u[:, p])
    gram = jnp.einsum(
        "tak,tal->tkl",
        image,
        image,
        precision=lax.Precision.HIGHEST,
        preferred_element_type=F32,
    )
    gram = gram + jnp.eye(gram.shape[1], dtype=F32)
    inverse = invert_factor(gram)
    basis = jnp.einsum(
        "tak,tlk->tal",
        image,
        inverse,
        precision=lax.Precision.HIGHEST,
        preferred_element_type=F32,
    )
    basis_out = (basis * jnp.sqrt(F32(width))).astype(BF16)
    basis_low = basis.astype(BF16)
    project = dot("tar,tak->trk", tile_u, basis_low).astype(BF16)
    coeff = dot("tar,trk->tak", tile_v, project)
    for p in range(panels):
        project = dot("tar,tak->trk", whole_u[p], basis_low).astype(BF16)
        inner = dot("trs,trk->tsk", cross[:, p], project).astype(BF16)
        coeff = coeff - dot("as,tsk->tak", side_u[p], inner)
    return basis_out[:, None], coeff.astype(BF16)[:, None]


def solution(mesh):
    in_specs = (
        P("row", "col", None, None),
        P("row", "col", None, None),
        P("row", "col"),
        P(None, "row", "col", None),
        P(None, "row", "col", None),
        P(None, "row"),
        P(None, "col", None),
        P("col"),
        P(),
    )
    out_specs = (P("row", "col", None, None), P("row", "col", None, None))
    return jax.shard_map(shards, mesh=mesh, in_specs=in_specs, out_specs=out_specs, check_vma=False)
```

time: 537 us -> 355 us (0.66)
  other arithmetic: 121 us -> 10.3 us
  waiting for transfers between devices: 317 us -> 249 us
  Pallas kernels: 0 us -> 14.3 us
  local copies, waits for them, and re-layouts: 21.9 us -> 9.95 us
  blocking collectives: 0 us -> 9.89 us
  matrix products: 55.4 us -> 45.7 us
    all_gather x3 -> x2, waiting for transfers between devices: 256 us -> 101 us  [the longest x1 52.5 us: shards(): whole_u = lax.all_gather(masked_panel, 'col', axis=2, tiled=True)]
    another operation x23 -> x0, other arithmetic: 113 us -> none  [the longest x14 69.9 us: update_tile(): factor = jnp.linalg.cholesky(gram)]
    unnamed x4 -> x5, waiting for transfers between devices: 1.41 us -> 81 us
    pallas_call x0 -> x1, Pallas kernels: none -> 14.3 us  [invert_factor(): pl.pallas_call(factor_kernel, grid=(tiles // step,), out_shape=jax.ShapeD...]
    unnamed x0 -> x1, blocking collectives: none -> 9.89 us
    another operation x20 -> x0, local copies, waits for them, and re-layouts: 8.12 us -> none  [the longest x15 7.95 us: update_tile(): lax.linalg.triangular_solve(factor, image, left_side=False, lower=True, t...]
    psum x1, waiting for transfers between devices: 59.9 us -> 67.1 us  [shards(): side_v = lax.psum(sides, 'row')]
    another operation x10 -> x0, matrix products: 6.91 us -> none  [the longest x6 5.97 us: update_tile(): lax.linalg.triangular_solve(factor, image, left_side=False, lower=True, t...]
  transfers between devices with their start and end apart: 4 -> 4, of which waited for: 4 -> 4; matrix products, arithmetic and copies ran while one was open for 2% -> 5% of each run, Pallas kernels for 0% -> 0%
where the time goes in v1:
time: 355 us; the launch traced here: 354 us
  waiting for transfers between devices  249 us (70%)
  matrix products  45.7 us (13%)
  between operations  14.5 us (4%)
  Pallas kernels  14.3 us (4%)
  other arithmetic  10.3 us (3%)
  local copies, waits for them, and re-layouts  9.95 us (3%)
  blocking collectives  9.89 us (3%)
    unnamed x5, waiting for transfers between devices  81 us
    psum x1, waiting for transfers between devices, shards(): side_v = lax.psum(sides, 'row')  67.1 us
    all_gather x1, waiting for transfers between devices, shards(): whole_u = lax.all_gather(masked_panel, 'col', axis=2, tiled=True)  52.5 us
    all_gather x1, waiting for transfers between devices, shards(): raw_v = lax.all_gather(panel_v, 'col', axis=2, tiled=True)  48.8 us
    dot_general x11, matrix products, dot(): return jnp.einsum(spec, a, b, preferred_element_type=F32)  38.1 us
    pallas_call x1, Pallas kernels, invert_factor(): pl.pallas_call(factor_kernel, grid=(tiles // step,), out_shape=jax.ShapeD...  14.3 us
    unnamed x1, blocking collectives  9.89 us
  transfers between devices with their start and end apart: 4, of which 4 were waited for; matrix products, arithmetic and copies ran while one was open for 5% of the time, Pallas kernels for 0%

profile of v1, /device:TPU:0, one launch (start us, length us, event | category | flops | bytes accessed | tf_op | source)
XLA Modules:
  0.0 354.2 jit_solution(2345518404819112041)
XLA Ops:
  7.2 0.0 copy-start
  7.2 0.0 copy-start.7
  7.2 0.0 all-gather.5.cloned.1.call-start
  7.2 0.7 all-gather.5.cloned.1.call-update
  7.9 0.0 all-gather.3.cloned.1.call-start
  8.0 0.8 compare_convert_fusion
  8.7 2.0 broadcast_multiply_fusion
  10.7 0.0 all-gather.3.cloned.1.call-update
  10.8 0.0 all-reduce.8.cloned.1.call-start
  11.5 0.6 fusion.43
  12.1 0.7 dynamic-update-slice
  12.8 9.9 %all-reduce = s32[4]{0:T(128)S(1)} all-reduce(s32[4]{0:T(128)S(1)} %dynamic-update-slice), channel_id=1, replica_groups=mesh['row'=8,'col'=4] {'col'}, use_global_device_ids=true, to_apply=%add | all-reduce | flops 4 | bytes 32
  22.7 48.8 %all-gather.5.cloned.1.call-done = bf16[2,2,1408,256]{3,2,1,0:T(8,128)(2,1)} async-done(((bf16[2,2,352,256]{3,2,1,0:T(8,128)(2,1)}), bf16[2,2,1408,256]{3,2,1,0:T(8,128)(2,1)}) %all-gather.5.cloned.1.call-update) | async-done | bytes 2883600 | tf_op jit(solution)/shard_map/all_gather | solution.py:114
  71.5 0.0 copy-done
  71.5 3.1 fusion.10
  74.6 1.7 gather_fusion
  76.3 2.7 select_select_fusion
  79.0 52.5 %all-gather.3.cloned.1.call-done = bf16[2,2,1408,256]{3,2,1,0:T(8,128)(2,1)} async-done(((bf16[2,2,352,256]{3,2,1,0:T(8,128)(2,1)}), bf16[2,2,1408,256]{3,2,1,0:T(8,128)(2,1)}) %all-gather.3.cloned.1.call-update) | async-done | bytes 2883600 | tf_op jit(solution)/shard_map/all_gather | solution.py:125
  131.5 2.6 select_bitcast_fusion
  134.1 0.0 all-reduce.8.cloned.1.call-update
  134.1 0.0 all-reduce.6.cloned.1.call-start
  134.1 67.1 %all-reduce.8.cloned.1.call-done = (bf16[4,2,352,256]{3,2,1,0:T(8,128)(2,1)}, bf16[2,1408,256]{2,1,0:T(8,128)(2,1)}) async-done(((bf16[4,2,352,256]{3,2,1,0:T(8,128)(2,1)}, bf16[2,1408,256]{2,1,0:T(8,128)(2,1)}), (bf16[4,2,352,256]{3,2,1,0:T(8,128)(2,1)}, bf16[2,1408,256]{2,1,0:T(8,128)(2,1)})) %all-reduce.8.cloned.1.call-update) | async-done | bytes 2883600 | tf_op jit(solution)/shard_map/psum | solution.py:122
  201.2 4.1 %convert_bitcast_fusion = bf16[4,2,2,256,256]{3,4,1,0,2:T(8,128)(2,1)} fusion(bf16[2,2,256,352]{2,3,1,0:T(8,128)(2,1)S(1)} %fusion.10, bf16[4,2,352,256]{3,2,1,0:T(8,128)(2,1)} %get-tuple-element.6), kind=kOutput, calls=%fused_computation.8 | convolution fusion | flops 739246080 | bytes 4259840 | tf_op jit(solution)/shard_map/tpar,cpas->ctprs/dot_general | solution.py:103
  205.3 0.0 all-reduce.6.cloned.1.call-update
  205.3 0.7 fusion.36
  206.0 0.1 compare_convert_fusion.1
  206.1 0.7 copy-done.3
  206.7 5.0 %fusion.15 = f32[2,1408,256]{2,1,0:T(8,128)} fusion(bf16[2,1,1408,256]{3,2,1,0:T(8,128)(2,1)S(1)} %copy-done.3, bf16[2,1,1408,256]{3,2,1,0:T(8,128)(2,1)} %param.10, bf16[1408,256]{1,0:T(8,128)(2,1)} %param.17, bf16[2,256]{1,0:T(2,128)(2,1)S(1)} %compare_convert_fusion.1), kind=kOutput, calls=%fused_computation.26 | convolution fusion | flops 739049472 | bytes 6489088 | tf_op jit(solution)/shard_map/tar,trk->tak/dot_general | solution.py:103
  211.7 80.2 %all-reduce.6.cloned.1.call-done = bf16[4,2,2,256,256]{3,4,1,0,2:T(8,128)(2,1)} async-done(((bf16[4,2,2,256,256]{3,4,1,0,2:T(8,128)(2,1)}), bf16[4,2,2,256,256]{3,4,1,0,2:T(8,128)(2,1)}) %all-reduce.6.cloned.1.call-update) | async-done | bytes 2097168
  291.9 2.5 dynamic-slice_bitcast_fusion
  294.4 3.3 fusion.18
  297.7 3.0 convolution_add_fusion.1
  300.8 0.1 copy-done.2
  300.9 0.1 copy-done.6
  301.0 0.6 convolution_add_fusion
  301.6 0.4 copy-done.5
  302.0 4.8 %convolution_add_fusion.2.gram_ref = f32[2,256,256]{2,1,0:T(8,128)S(1)} fusion(f32[2,1408,256]{2,1,0:T(8,128)S(1)} %convolution_add_fusion, f32[256,256]{1,0:T(8,128)S(1)} %copy-done.5), kind=kOutput, calls=%fused_computation.29 | convolution fusion | flops 2214723584 | bytes 3670016 | tf_op jit(solution)/shard_map/tak,tal->tkl/dot_general | solution.py:142
  306.8 14.3 %shard_map.104 = f32[2,256,256]{2,1,0:T(8,128)S(1)} custom-call(f32[2,256,256]{2,1,0:T(8,128)S(1)} %convolution_add_fusion.2.gram_ref), custom_call_target="tpu_custom_call" | custom-call | flops 33554432 | bytes 1048576 | tf_op jit(solution)/shard_map/pallas_call | solution.py:89
  321.1 2.8 fusion.44
  323.9 1.6 copy-done.1
  325.5 1.5 fusion.4
  327.0 5.0 %fusion.6 = f32[2,256,1408]{2,1,0:T(8,128)} fusion(bf16[2,1,1408,256]{3,2,1,0:T(8,128)(2,1)} %param.10, bf16[2,1,1408,256]{3,2,1,0:T(8,128)(2,1)S(1)} %copy-done.3, bf16[2,256]{1,0:T(2,128)(2,1)S(1)} %compare_convert_fusion.1, f32[2,1408,256]{2,1,0:T(8,128)} %copy-done.1), kind=kOutput, calls=%fused_computation.15 | convolution fusion | flops 739770368 | bytes 8651776 | tf_op jit(solution)/shard_map/tar,trk->tak/dot_general | solution.py:103
  331.9 3.2 convolution_convert_fusion.2
  335.2 0.0 copy-start.4
  335.2 4.3 %convolution_subtract_fusion.1 = f32[2,256,1408]{2,1,0:T(8,128)} fusion(f32[2,256,1408]{2,1,0:T(8,128)} %fusion.6, bf16[2,256,256]{1,2,0:T(8,128)(2,1)S(1)} %convolution_convert_fusion.2, bf16[2,1408,256]{2,1,0:T(8,128)(2,1)} %get-tuple-element.7), kind=kOutput, calls=%fused_computation.2 | convolution fusion | flops 369819648 | bytes 6750208 | tf_op jit(solution)/shard_map/as,tsk->tak/dot_general | solution.py:103
  339.5 3.9 %convolution_convert_fusion.1 = bf16[2,256,256]{1,2,0:T(8,128)(2,1)} fusion(bf16[2,2,1408,256]{3,2,1,0:T(8,128)(2,1)} %all-gather.3.cloned.1.call-done, bf16[2,2,256,256]{2,3,0,1:T(8,128)(2,1)S(1)} %copy-done.4, f32[2,1408,256]{2,1,0:T(8,128)} %copy-done.1), kind=kOutput, calls=%fused_computation.34 | convolution fusion | flops 437190656 | bytes 4849664 | tf_op jit(solution)/shard_map/trs,trk->tsk/dot_general | solution.py:103
  343.4 2.7 fusion.1
  346.1 1.6 copy.22
  (13 shorter events, 0.0 us)
Async XLA Ops:
  7.2 64.3 %copy-start = (bf16[2,352,1408]{2,1,0:T(8,128)(2,1)S(1)}, bf16[2,352,1408]{2,1,0:T(8,128)(2,1)}, u32[]{:S(2)}) copy-start(bf16[2,352,1408]{2,1,0:T(8,128)(2,1)} %param.15) | copy-start | bytes 5947396
  7.2 4.3 %copy-start.7 = (u32[32]{0:T(128)S(1)}, u32[32]{0:T(128)}, u32[]{:S(2)}) copy-start(u32[32]{0:T(128)} %constant.62) | copy-start | bytes 388
  7.2 64.3 %all-gather.5.cloned.1.call-start = ((), (), s32[]{:S(2)}) async-start(), calls=%async_computation.1 | async-start | bytes 3604480 | tf_op jit(solution)/shard_map/all_gather | solution.py:114
  7.9 123.6 %all-gather.3.cloned.1.call-start = ((), (), s32[]{:S(2)}) async-start(), calls=%async_computation | async-start | bytes 3604480 | tf_op jit(solution)/shard_map/all_gather | solution.py:125
  10.8 190.4 %all-reduce.8.cloned.1.call-start = ((), (), s32[]{:S(2)}) async-start(), calls=%async_computation.3 | async-start | bytes 5767168 | tf_op jit(solution)/shard_map/psum | solution.py:122
  134.1 157.8 %all-reduce.6.cloned.1.call-start = ((), (), s32[]{:S(2)}) async-start(), calls=%async_computation.2 | async-start | bytes 4194304
  205.3 0.7 copy-start.8
  205.3 1.5 copy-start.3
  297.7 3.2 copy-start.2
  297.7 3.3 copy-start.6
  301.0 0.9 copy-start.5
  323.9 1.6 copy-start.1
  335.2 4.3 %copy-start.4 = (bf16[2,2,256,256]{2,3,0,1:T(8,128)(2,1)S(1)}, bf16[2,2,256,256]{2,3,0,1:T(8,128)(2,1)}, u32[]{:S(2)}) copy-start(bf16[2,2,256,256]{2,3,0,1:T(8,128)(2,1)} %dynamic-slice_bitcast_fusion) | copy-start | bytes 1572868
Sparse Core Ops, SparseCore 0:
  9.6 61.8 all-gather.4
  73.6 57.8 all-gather.2
  135.4 65.7 all-reduce.7
  205.4 86.4 all-reduce.5

commit v2 on v1

--- a/solution.py
+++ b/solution.py
@@ -1,3 +1,5 @@
+import functools
+
 import jax
 import jax.numpy as jnp
 from jax import lax
@@ -99,46 +101,249 @@
     )(gram)
 
 
+def exchange_kernel(
+    n_row, n_col, v_ref, u_ref, inv_ref, goal_ref,
+    u_all, s_all, side_u, side_v,
+    v_all, acc_u, acc_v, core_u, core_v, step_u, step_v,
+    v_send, v_recv, u_send, u_recv, s_send, s_recv,
+    ru_send, ru_recv, rv_send, rv_recv,
+):
+    row = lax.axis_index("row")
+    col = lax.axis_index("col")
+    panels, tiles, height, rank = v_ref.shape
+    half = n_col // 2
+    quarter = half // 2
+    bits = [1 << k for k in range(1, n_row.bit_length() - 1)]
+
+    def across(bit):
+        return row + bit * (1 - 2 * lax.rem(row // bit, 2))
+
+    def remote(src, dst, send, recv, **where):
+        return pltpu.make_async_remote_copy(
+            src_ref=src, dst_ref=dst, send_sem=send, recv_sem=recv,
+            device_id=where, device_id_type=pl.DeviceIdType.MESH,
+        )
+
+    barrier = pltpu.get_barrier_semaphore()
+    for d in range(1, n_col):
+        pl.semaphore_signal(
+            barrier, inc=1, device_id={"col": lax.rem(col + d, n_col)},
+            device_id_type=pl.DeviceIdType.MESH,
+        )
+    for bit in [1] + bits:
+        pl.semaphore_signal(
+            barrier, inc=1, device_id={"row": across(bit)},
+            device_id_type=pl.DeviceIdType.MESH,
+        )
+    pl.semaphore_wait(barrier, n_col - 1 + 1 + len(bits))
+
+    def hop(whole, send, recv, s):
+        right = remote(
+            whole.at[jnp.maximum(col - s, 0)], whole.at[jnp.maximum(col - s, 0)],
+            send.at[0, s], recv.at[0, s], col=jnp.minimum(col + 1, n_col - 1),
+        )
+        left = remote(
+            whole.at[jnp.minimum(col + s, n_col - 1)], whole.at[jnp.minimum(col + s, n_col - 1)],
+            send.at[1, s], recv.at[1, s], col=jnp.maximum(col - 1, 0),
+        )
+        return right, left
+
+    def hop_start(whole, send, recv, s):
+        right, left = hop(whole, send, recv, s)
+
+        @pl.when((col - s >= 0) & (col + 1 < n_col))
+        def _():
+            right.start()
+
+        @pl.when((col + s < n_col) & (col >= 1))
+        def _():
+            left.start()
+
+    def hop_recv(whole, send, recv, s):
+        right, left = hop(whole, send, recv, s)
+
+        @pl.when(col - 1 - s >= 0)
+        def _():
+            right.wait_recv()
+
+        @pl.when(col + 1 + s < n_col)
+        def _():
+            left.wait_recv()
+
+    def hop_end(whole, send, recv, s):
+        right, left = hop(whole, send, recv, s)
+
+        @pl.when((col - s >= 0) & (col + 1 < n_col))
+        def _():
+            right.wait_send()
+
+        @pl.when((col + s < n_col) & (col >= 1))
+        def _():
+            left.wait_send()
+
+    v_all[col] = v_ref[...]
+    for s in range(n_col - 1):
+        hop_start(v_all, v_send, v_recv, s)
+        if s == 0:
+            u_all[col] = u_ref[...]
+        hop_recv(v_all, v_send, v_recv, s)
+    for s in range(n_col - 1):
+        hop_end(v_all, v_send, v_recv, s)
+
+    hop_start(u_all, u_send, u_recv, 0)
+    for p in range(panels):
+        for t in range(tiles):
+            raw = jnp.concatenate([v_all[z, p, t] for z in range(n_col)], axis=0)
+            s_all[col, p, t] = jnp.dot(
+                inv_ref[p], raw, preferred_element_type=F32
+            ).astype(BF16)
+    for s in range(n_col - 2):
+        hop_recv(u_all, u_send, u_recv, s)
+        hop_start(u_all, u_send, u_recv, s + 1)
+    hop_start(s_all, s_send, s_recv, 0)
+    hop_recv(u_all, u_send, u_recv, n_col - 2)
+    for s in range(n_col - 1):
+        hop_end(u_all, u_send, u_recv, s)
+
+    def chosen(goal, source):
+        total = None
+        for t in range(tiles):
+            hit = jnp.where(goal[0:1, :] == row * tiles + t, 1.0, 0.0)
+            term = source[t].astype(F32) * hit
+            total = term if total is None else total + term
+        return total.astype(BF16)
+
+    def pick(acc, whole):
+        goal = goal_ref[...]
+        for z in range(n_col):
+            for p in range(panels):
+                acc[z, p] = chosen(goal, [whole[z, p, t] for t in range(tiles)])
+
+    def spread(acc, out, core_buf, step_buf, send, recv, between):
+        core = lax.rem(row, 2)
+        mine = core * half
+        first = remote(
+            acc.at[pl.ds((1 - core) * half, half)], core_buf, send.at[0], recv.at[0],
+            row=across(1),
+        )
+        first.start()
+        first.wait()
+        for k in range(half):
+            acc[mine + k] = acc[mine + k] + core_buf[k]
+        for step, bit in enumerate(bits):
+            copies = []
+            for piece in range(2):
+                to = bit if piece == 0 else bits[len(bits) - 1 - step]
+                copies.append(
+                    remote(
+                        acc.at[pl.ds(mine + piece * quarter, quarter)],
+                        step_buf.at[step, piece],
+                        send.at[1 + 2 * step + piece],
+                        recv.at[1 + 2 * step + piece],
+                        row=across(to),
+                    )
+                )
+                copies[-1].start()
+            between(step)
+            for piece in range(2):
+                copies[piece].wait()
+                for k in range(quarter):
+                    at = mine + piece * quarter + k
+                    acc[at] = acc[at] + step_buf[step, piece, k]
+        last = remote(
+            acc.at[pl.ds(mine, half)], out.at[pl.ds(mine, half)],
+            send.at[1 + 2 * len(bits)], recv.at[1 + 2 * len(bits)], row=across(1),
+        )
+        last.start()
+        for k in range(half):
+            out[mine + k] = acc[mine + k]
+        last.wait()
+
+    def next_hop(step):
+        if step + 1 < n_col - 1:
+            hop_recv(s_all, s_send, s_recv, step)
+            hop_start(s_all, s_send, s_recv, step + 1)
+
+    pick(acc_u, u_all)
+    spread(acc_u, side_u, core_u, step_u, ru_send, ru_recv, next_hop)
+    for s in range(len(bits), n_col - 1):
+        if s > len(bits):
+            hop_start(s_all, s_send, s_recv, s)
+        hop_recv(s_all, s_send, s_recv, s)
+    for s in range(n_col - 1):
+        hop_end(s_all, s_send, s_recv, s)
+    pick(acc_v, s_all)
+    spread(acc_v, side_v, core_v, step_v, rv_send, rv_recv, lambda step: None)
+
+
+def exchange(n_row, n_col, panel_v, masked_panel, inverse_block, column_tiles):
+    panels, tiles, height, rank = panel_v.shape
+    goal = jnp.broadcast_to(column_tiles.reshape(1, 1), (8, rank)).astype(jnp.int32)
+    half, quarter = n_col // 2, n_col // 4
+    steps = n_row.bit_length() - 2
+    side = (n_col, panels, height, rank)
+    dma = pltpu.SemaphoreType.DMA
+    vmem = pl.BlockSpec(memory_space=pltpu.VMEM)
+    spread_buffers = [
+        pltpu.VMEM((half,) + side[1:], BF16),
+        pltpu.VMEM((steps, 2, quarter) + side[1:], BF16),
+    ]
+    return pl.pallas_call(
+        lambda *refs: exchange_kernel(n_row, n_col, *refs),
+        out_shape=[
+            jax.ShapeDtypeStruct((n_col,) + panel_v.shape, BF16),
+            jax.ShapeDtypeStruct((n_col,) + panel_v.shape, BF16),
+            jax.ShapeDtypeStruct(side, BF16),
+            jax.ShapeDtypeStruct(side, BF16),
+        ],
+        in_specs=[vmem] * 4,
+        out_specs=[vmem] * 4,
+        scratch_shapes=[
+            pltpu.VMEM((n_col,) + panel_v.shape, BF16),
+            pltpu.VMEM(side, BF16),
+            pltpu.VMEM(side, BF16),
+            spread_buffers[0],
+            spread_buffers[0],
+            spread_buffers[1],
+            spread_buffers[1],
+        ]
+        + [dma((2, n_col - 1))] * 6
+        + [dma((2 + 2 * steps,))] * 4,
+        compiler_params=pltpu.CompilerParams(
+            collective_id=0, has_side_effects=True, vmem_limit_bytes=60 * 1024 * 1024
+        ),
+    )(panel_v, masked_panel, inverse_block, goal)
+
+
 def dot(spec, a, b):
     return jnp.einsum(spec, a, b, preferred_element_type=F32)
 
 
 def shards(
+    n_row, n_col,
     slab_u, slab_v, slab_rank, panel_u, panel_v, panel_rank, inverse_block, column_tiles, sketch
 ):
-    rows_here = panel_u.shape[1]
+    tiles = panel_u.shape[1]
     panels = panel_u.shape[0]
-    width = sketch.shape[0]
-    me = lax.axis_index("row")
-    targets = lax.all_gather(column_tiles, "col", axis=0, tiled=True)
-    raw_v = lax.all_gather(panel_v, "col", axis=2, tiled=True)
+    width, rank = sketch.shape
     masked_panel = mask_columns(panel_u, panel_rank[:, :, None, None])
-    solved = dot("pab,ptbr->tpar", inverse_block, raw_v).astype(BF16)
-    owner = targets // rows_here
-    local = targets - owner * rows_here
-    sides = jnp.where(
-        (owner == me)[:, None, None, None], jnp.take(solved, local, axis=0), jnp.zeros((), BF16)
-    )
-    side_v = lax.psum(sides, "row")
-    part = dot("tpar,cpas->ctprs", solved, side_v).astype(BF16)
-    cross = lax.psum_scatter(part, "col", scatter_dimension=0, tiled=True)[0]
-    whole_u = lax.all_gather(masked_panel, "col", axis=2, tiled=True)
-    target = column_tiles[0]
-    mine = target // rows_here
-    pick_u = lax.dynamic_index_in_dim(
-        whole_u, target - mine * rows_here, 1, keepdims=False
-    )
-    side_u = lax.psum(jnp.where(mine == me, pick_u, jnp.zeros_like(pick_u)), "row")
-
-    side_small = dot("pas,ak->psk", side_u, sketch).astype(BF16)
+    u_all, s_all, side_u, side_v = exchange(
+        n_row, n_col, panel_v, masked_panel, inverse_block, column_tiles
+    )
+    whole_u = u_all.transpose(1, 2, 0, 3, 4).reshape(panels, tiles, width, rank)
+    side_u = side_u.transpose(1, 0, 2, 3).reshape(panels, width, rank)
+    whole_s = s_all.transpose(1, 2, 0, 3, 4).reshape(panels, tiles, width, rank)
+    side_v = side_v.transpose(1, 0, 2, 3).reshape(panels, width, rank)
+    cross = dot("ptar,pas->ptrs", whole_s, side_v).astype(BF16)
+    update = dot("pas,ptrs->ptar", side_u, cross).astype(BF16)
     tile_u = slab_u[:, 0]
     tile_v = slab_v[:, 0]
     tile_u = mask_columns(tile_u, slab_rank[:, 0][:, None, None])
     small_v = dot("tar,ak->trk", tile_v, sketch).astype(BF16)
-    small_u = (-dot("tprs,psk->tprk", cross, side_small)).astype(BF16)
+    small_u = (-dot("ptar,ak->ptrk", update, sketch)).astype(BF16)
     image = dot("tar,trk->tak", tile_u, small_v)
     for p in range(panels):
-        image = image + dot("tar,trk->tak", whole_u[p], small_u[:, p])
+        image = image + dot("tar,trk->tak", whole_u[p], small_u[p])
     gram = jnp.einsum(
         "tak,tal->tkl",
         image,
@@ -161,8 +366,7 @@
     coeff = dot("tar,trk->tak", tile_v, project)
     for p in range(panels):
         project = dot("tar,tak->trk", whole_u[p], basis_low).astype(BF16)
-        inner = dot("trs,trk->tsk", cross[:, p], project).astype(BF16)
-        coeff = coeff - dot("as,tsk->tak", side_u[p], inner)
+        coeff = coeff - dot("tar,trk->tak", update[p], project)
     return basis_out[:, None], coeff.astype(BF16)[:, None]
 
 
@@ -179,4 +383,5 @@
         P(),
     )
     out_specs = (P("row", "col", None, None), P("row", "col", None, None))
-    return jax.shard_map(shards, mesh=mesh, in_specs=in_specs, out_specs=out_specs, check_vma=False)
+    body = functools.partial(shards, mesh.shape["row"], mesh.shape["col"])
+    return jax.shard_map(body, mesh=mesh, in_specs=in_specs, out_specs=out_specs, check_vma=False)

time: 355 us -> 254 us (0.72)
  waiting for transfers between devices: 249 us -> 0 us
  Pallas kernels: 14.3 us -> 191 us
  between operations: 14.5 us -> 1.4 us
  blocking collectives: 9.89 us -> 0 us
  other arithmetic: 10.3 us -> 6.18 us
    pallas_call x0 -> x1, Pallas kernels: none -> 177 us  [exchange(): pl.pallas_call(lambda *refs: exchange_kernel(n_row, n_col, *refs), out_sh...]
    all_gather x2 -> x0, waiting for transfers between devices: 101 us -> none  [the longest x1 52.5 us: shards(): whole_u = lax.all_gather(masked_panel, 'col', axis=2, tiled=True)]
    unnamed x5 -> x0, waiting for transfers between devices: 81 us -> none
    psum x1 -> x0, waiting for transfers between devices: 67.1 us -> none  [shards(): side_v = lax.psum(sides, 'row')]
    unnamed x1 -> x0, blocking collectives: 9.89 us -> none
    select_n x2 -> x0, other arithmetic: 5.24 us -> none  [the longest x1 2.69 us: shards(): jnp.where((owner == me)[:, None, None, None], jnp.take(solved, local, axi...]
    transpose x0 -> x3, local copies, waits for them, and re-layouts: none -> 5 us  [the longest x1 3.72 us: shards(): whole_s = s_all.transpose(1, 2, 0, 3, 4).reshape(panels, tiles, width, rank)]
    dot_general x11 -> x8, matrix products: 38.1 us -> 33.5 us  [dot(): return jnp.einsum(spec, a, b, preferred_element_type=F32)]
  transfers between devices with their start and end apart: 4 -> 0, of which waited for: 4 -> 0; matrix products, arithmetic and copies ran while one was open for 5% -> 0% of each run, Pallas kernels for 0% -> 0%
where the time goes in v2:
time: 254 us; the launch traced here: 253 us
  Pallas kernels  191 us (75%)
  matrix products  42.9 us (17%)
  local copies, waits for them, and re-layouts  11.4 us (4%)
  other arithmetic  6.18 us (2%)
    pallas_call x1, Pallas kernels, exchange(): pl.pallas_call(lambda *refs: exchange_kernel(n_row, n_col, *refs), out_sh...  177 us
    dot_general x8, matrix products, dot(): return jnp.einsum(spec, a, b, preferred_element_type=F32)  33.5 us
    pallas_call x1, Pallas kernels, invert_factor(): pl.pallas_call(factor_kernel, grid=(tiles // step,), out_shape=jax.ShapeD...  14.1 us

profile of v2, /device:TPU:0, one launch (start us, length us, event | category | flops | bytes accessed | tf_op | source)
XLA Modules:
  0.0 253.2 jit_solution(15561042870702179052)
XLA Ops:
  0.6 0.0 copy-start
  0.6 0.9 compare_convert_fusion
  1.5 2.0 broadcast_multiply_fusion.refs_1_
  4.2 0.6 broadcast_in_dim.18.refs_3_
  4.8 177.1 %shard_map.104 = (bf16[4,2,2,352,256]{4,3,2,1,0:T(8,128)(2,1)}, bf16[4,2,2,352,256]{4,3,2,1,0:T(8,128)(2,1)}, bf16[4,2,352,256]{3,2,1,0:T(8,128)(2,1)}, bf16[4,2,352,256]{3,2,1,0:T(8,128)(2,1)}) custom-call(bf16[2,2,352,256]{3,2,1,0:T(8,128)(2,1)} %refs_0_.1, bf16[2,2,352,256]{3,2,1,0:T(8,128)(2,1)} %broadcast_multiply_fusion.refs_1_, ...), custom_call_target="tpu_custom_call" | custom-call | tf_op jit(solution)/shard_map/pallas_call | solution.py:291
  181.9 0.0 copy-start.5
  181.9 3.7 %copy.18 = bf16[2,2,4,352,256]{4,3,2,1,0:T(8,128)(2,1)} copy(bf16[2,2,4,352,256]{4,3,1,0,2:T(8,128)(2,1)} %bitcast.88) | data formatting | bytes 5767168 | tf_op jit(solution)/shard_map/transpose | solution.py:335
  185.6 0.0 copy-done.5
  185.7 0.0 copy-start.4
  185.7 0.1 copy.19
  185.8 1.3 copy-done.4
  187.0 1.2 copy.20
  188.2 5.7 %fusion = bf16[2,2,1408,256]{2,3,1,0:T(8,128)(2,1)} fusion(bf16[2,1408,256,1]{2,1,3,0:T(8,128)(2,1)} %bitcast.86, bf16[2,2,1408,256]{3,2,1,0:T(8,128)(2,1)} %bitcast.84, bf16[2,1408,256,1]{2,1,3,0:T(8,128)(2,1)S(1)} %bitcast.85), kind=kOutput, calls=%fused_computation.5 | convolution fusion | flops 1478098944 | bytes 8650752 | tf_op jit(solution)/shard_map/pas,ptrs->ptar/dot_general | solution.py:319
  193.9 0.0 copy-start.3
  193.9 3.1 %fusion.7 = bf16[2,2,256,256]{3,2,1,0:T(8,128)(2,1)S(1)} fusion(bf16[2,2,1408,256]{2,3,1,0:T(8,128)(2,1)} %fusion, bf16[1408,256]{1,0:T(8,128)(2,1)} %param.17), kind=kOutput, calls=%fused_computation.18 | convolution fusion | flops 738721792 | bytes 4128768 | tf_op jit(solution)/shard_map/ptar,ak->ptrk/dot_general | solution.py:319
  197.0 0.0 copy-done.3
  197.0 1.3 fusion.29
  198.3 0.0 copy-start.6
  198.3 0.1 copy.17
  198.4 0.0 copy-start.1
  198.4 0.5 copy-done.6
  199.0 0.1 compare_convert_fusion.1
  199.0 0.0 copy-done
  199.0 5.0 %fusion.9 = f32[2,1408,256]{2,1,0:T(8,128)} fusion(bf16[2,1,1408,256]{3,2,1,0:T(8,128)(2,1)} %param.9, bf16[2,1,1408,256]{3,2,1,0:T(8,128)(2,1)S(1)} %copy-done, bf16[1408,256]{1,0:T(8,128)(2,1)} %param.17, bf16[2,256]{1,0:T(2,128)(2,1)S(1)} %compare_convert_fusion.1), kind=kOutput, calls=%fused_computation.21 | convolution fusion | flops 739049472 | bytes 6489088 | tf_op jit(solution)/shard_map/tar,trk->tak/dot_general | solution.py:319
  204.0 0.0 copy-done.1
  204.0 0.0 copy-start.2
  204.0 2.5 convolution_add_fusion.1
  206.5 0.0 copy-done.2
  206.5 0.1 copy.21
  206.6 0.6 convolution_add_fusion
  207.2 5.0 %convolution_add_fusion.2.gram_ref = f32[2,256,256]{2,1,0:T(8,128)S(1)} fusion(f32[2,1408,256]{2,1,0:T(8,128)S(1)} %convolution_add_fusion, f32[256,256]{1,0:T(8,128)S(1)} %fusion.22), kind=kOutput, calls=%fused_computation.22 | convolution fusion | flops 2214723584 | bytes 3670016 | tf_op jit(solution)/shard_map/tak,tal->tkl/dot_general | solution.py:347
  212.2 14.1 %shard_map.105 = f32[2,256,256]{2,1,0:T(8,128)S(1)} custom-call(f32[2,256,256]{2,1,0:T(8,128)S(1)} %convolution_add_fusion.2.gram_ref), custom_call_target="tpu_custom_call" | custom-call | flops 33554432 | bytes 1048576 | tf_op jit(solution)/shard_map/pallas_call | solution.py:91
  226.3 4.4 %fusion.30 = f32[2,1408,256]{2,1,0:T(8,128)} fusion(f32[2,1408,256]{2,1,0:T(8,128)S(1)} %convolution_add_fusion, f32[2,256,256]{2,1,0:T(8,128)S(1)} %shard_map.105), kind=kOutput, calls=%fused_computation.42 | convolution fusion | flops 2214592512 | bytes 6291456 | tf_op jit(solution)/shard_map/tak,tlk->tal/dot_general | solution.py:356
  230.8 4.9 %convolution_bitcast_fusion = f32[2,1408,256]{1,2,0:T(8,128)} fusion(bf16[2,1,1408,256]{3,2,1,0:T(8,128)(2,1)S(1)} %copy-done, bf16[2,1,1408,256]{3,2,1,0:T(8,128)(2,1)} %param.9, bf16[2,256]{1,0:T(2,128)(2,1)S(1)} %compare_convert_fusion.1, f32[2,1408,256]{2,1,0:T(8,128)} %fusion.30), kind=kOutput, calls=%fused_computation.6 | convolution fusion | flops 739770368 | bytes 8651776 | tf_op jit(solution)/shard_map/tar,trk->tak/dot_general | solution.py:319
  235.7 6.4 %convolution_subtract_fusion.1 = f32[2,1408,256]{1,2,0:T(8,128)} fusion(f32[2,1408,256]{1,2,0:T(8,128)} %convolution_bitcast_fusion, bf16[2,2,1408,256]{2,3,1,0:T(8,128)(2,1)} %fusion, bf16[2,1408,256]{2,1,0:T(8,128)(2,1)} %bitcast.83, f32[2,1408,256]{2,1,0:T(8,128)} %fusion.30), kind=kOutput, calls=%fused_computation.2 | convolution fusion | flops 739770368 | bytes 11534336 | tf_op jit(solution)/shard_map/tar,trk->tak/dot_general | solution.py:319
  242.1 5.4 %fusion.2 = bf16[2,1,1408,256]{2,3,0,1:T(8,128)(2,1)} fusion(f32[2,1408,256]{1,2,0:T(8,128)} %convolution_subtract_fusion.1, bf16[2,2,1408,256]{2,3,1,0:T(8,128)(2,1)} %fusion, bf16[2,1408,256]{2,1,0:T(8,128)(2,1)S(1)} %bitcast.81, f32[2,1408,256]{2,1,0:T(8,128)} %fusion.30), kind=kOutput, calls=%fused_computation.9 | convolution fusion | flops 740491264 | bytes 10092544 | tf_op jit(solution)/shard_map/tar,trk->tak/dot_general | solution.py:319
  247.5 2.5 copy.27
  250.0 3.2 %fusion.3 = bf16[2,1,1408,256]{3,2,1,0:T(8,128)(2,1)} fusion(f32[2,1408,256]{2,1,0:T(8,128)} %fusion.30), kind=kLoop, calls=%fused_computation.10 | loop fusion | flops 1441792 | bytes 4325376
  (1 shorter events, 0.0 us)
Async XLA Ops:
  0.6 198.4 %copy-start = (bf16[2,1,1408,256]{3,2,1,0:T(8,128)(2,1)S(1)}, bf16[2,1,1408,256]{3,2,1,0:T(8,128)(2,1)}, u32[]{:S(2)}) copy-start(bf16[2,1,1408,256]{3,2,1,0:T(8,128)(2,1)} %param.10) | copy-start | bytes 4325380
  181.9 3.7 %copy-start.5 = (bf16[4,2,352,256]{3,2,1,0:T(8,128)(2,1)S(1)}, bf16[4,2,352,256]{3,2,1,0:T(8,128)(2,1)}, u32[]{:S(2)}) copy-start(bf16[4,2,352,256]{3,2,1,0:T(8,128)(2,1)} %get-tuple-element.8) | copy-start | bytes 4325380
  185.7 1.4 copy-start.4
  193.9 3.1 %copy-start.3 = (bf16[4,2,2,352,256]{4,3,2,1,0:T(8,128)(2,1)S(1)}, bf16[4,2,2,352,256]{4,3,2,1,0:T(8,128)(2,1)}, u32[]{:S(2)}) copy-start(bf16[4,2,2,352,256]{4,3,2,1,0:T(8,128)(2,1)} %get-tuple-element.6) | copy-start | bytes 8650756
  198.3 0.7 copy-start.6
  198.4 5.6 %copy-start.1 = (bf16[1,2,4,352,256]{4,3,2,1,0:T(8,128)(2,1)}, bf16[1,2,4,352,256]{4,3,2,1,0:T(8,128)(2,1)S(1)}, u32[]{:S(2)}) copy-start(bf16[1,2,4,352,256]{4,3,2,1,0:T(8,128)(2,1)S(1)} %copy.17) | copy-start | bytes 4325380
  204.0 2.5 copy-start.2
